TPU v7x, 32 devices: a whole 2x2x4 slice. The times are simulated.
32 devices in a mesh: groups: 2 (over y), dp: 4 (over z), section: 2 (over x), tensor: 2 (over core).
Axes of the slice: x: 2, y: 2, z: 4, core: 2. Of those that a mesh axis runs over, the one named last changes fastest.
Arguments:
- cotangent: bfloat16 [2, 1024, 2048], P('section', ('groups', 'dp')), parts along dimension 1, may hold values from -6 to 6
- routes: int32 [2, 8, 2], P('section', ('groups', 'dp')), parts along dimension 1, may hold values from 0 to 3, all different within a row
- gate_values: float32 [2, 1024, 2], P('section', ('groups', 'dp')), parts along dimension 1, may hold values from 0.1 to 0.9
- up_weight: bfloat16 [2, 4, 2048, 7168], P('section', 'dp', None, 'tensor'), may hold values from -0.125 to 0.125
- down_weight: bfloat16 [2, 4, 7168, 2048], P('section', 'dp', 'tensor'), may hold values from -0.0625 to 0.0625
- pre_activation: bfloat16 [2, 8, 4, 128, 7168], P('section', ('groups', 'dp'), None, None, 'tensor'), parts along dimension 1, may hold values from -6 to 6
- input_sketch: float32 [2, 1024, 64], P('section', ('groups', 'dp')), parts along dimension 1, may hold values from -6 to 6
- model_sketch: bfloat16 [2, 2048, 64], P('section'), may hold values from -0.125 to 0.125
- hidden_sketch: bfloat16 [2, 4, 7168, 64], P('section', 'dp', 'tensor'), may hold values from -0.0625 to 0.0625
- lengths: int32 [2, 8, 4], P('section', ('groups', 'dp')), parts along dimension 1, may hold values from 1 to 64, 128 in all within a row
Outputs:
- handed: bfloat16 [2, 1024, 2048], P('section', ('groups', 'dp')), parts along dimension 1
- features: float32 [2, 32, 64, 128], P('section', ('groups', 'dp')), parts along dimension 1
There are 2 independent parts, one for each index of `groups`. A program takes and returns all parts, laid end to end along the dimension named above; an argument that names none is the same for every part. Nothing has to cross between parts.
Inputs may be any that keep to these rules, and one draw needn't show every extreme that they name: `routes`: the two experts of a block differ. `lengths`: each row of counts sums to 128, and its largest is 64.
All inputs are finite; a program needn't handle non-finite values.
Results may differ from a plain program's by a relative error of at most 0.0037.
Values may be sent and summed in bfloat16 or wider, within the bound.
No kernel may reach another device: no remote copies, remote signals or barrier semaphores. Data moves between devices by JAX's collectives and lax.ppermute only.
A program may use at most 128 MiB of HBM per device.

v0:
```python
import functools

import jax
import jax.numpy as jnp
from jax import lax
from jax.experimental import pallas as pl
from jax.experimental.pallas import tpu as pltpu
from jax.sharding import PartitionSpec as P

EXPERTS = 4
CHUNKS = 2
AHEAD = 2
NT = (((1,), (1,)), ((), ()))


def xored(block, axis, bits):
    n = lax.axis_size(axis)
    return lax.ppermute(block, axis, [(i, i ^ bits) for i in range(n)])


ANYWHERE = pl.BlockSpec(memory_space=pl.ANY)
RESIDENT = pl.BlockSpec(memory_space=pltpu.VMEM)


def held_kernel(block_ref, *refs):
    refs[-1][...] = block_ref[...]


def held(block, *events):
    return pl.pallas_call(
        held_kernel,
        in_specs=[RESIDENT] + [ANYWHERE] * len(events),
        out_specs=RESIDENT,
        out_shape=jax.ShapeDtypeStruct(block.shape, block.dtype),
        compiler_params=pltpu.CompilerParams(vmem_limit_bytes=1 << 20),
        name="held",
    )(block, *events)


def merge_kernel(keep_ref, came_ref, own_ref, *sent_refs):
    rows = own_ref.shape[0]
    own_ref[...] = keep_ref[:rows] + came_ref[:rows].astype(jnp.float32)
    for at, sent_ref in enumerate(sent_refs):
        part = slice((at + 1) * rows, (at + 2) * rows)
        total = keep_ref[part] + came_ref[part].astype(jnp.float32)
        sent_ref[...] = total.astype(jnp.bfloat16)


def merged(keep, came, rows):
    count, wide = keep.shape
    others = count // rows - 1
    return pl.pallas_call(
        merge_kernel,
        in_specs=[RESIDENT] * 2,
        out_specs=[RESIDENT] * (1 + others),
        out_shape=[jax.ShapeDtypeStruct((rows, wide), jnp.float32)]
        + [jax.ShapeDtypeStruct((rows, wide), jnp.bfloat16)] * others,
        compiler_params=pltpu.CompilerParams(vmem_limit_bytes=4 << 20),
        cost_estimate=pl.CostEstimate(
            flops=count * wide, bytes_accessed=8 * count * wide, transcendentals=0
        ),
        name="merge",
    )(keep, came)


def finish_kernel(slots, own_ref, cot_ref, weight_ref, *refs):
    grad_ref, vec_ref = refs[-2:]
    width = grad_ref.shape[1]
    total = weight_ref[:, :1] * own_ref[...]
    for slot in range(1, slots):
        total += weight_ref[:, slot : slot + 1] * refs[slot - 1][...].astype(jnp.float32)
    grad_ref[...] = (cot_ref[...].astype(jnp.float32) + total[:, :width]).astype(jnp.bfloat16)
    vec_ref[...] = total[:, width:]


def finished(own, cot, weight, backs, *events):
    rows, wide = own.shape
    width = cot.shape[1]
    return pl.pallas_call(
        functools.partial(finish_kernel, 1 + len(backs)),
        in_specs=[RESIDENT] * (3 + len(backs)) + [ANYWHERE] * len(events),
        out_specs=[RESIDENT] * 2,
        out_shape=[
            jax.ShapeDtypeStruct((rows, width), jnp.bfloat16),
            jax.ShapeDtypeStruct((rows, wide - width), jnp.float32),
        ],
        compiler_params=pltpu.CompilerParams(vmem_limit_bytes=4 << 20),
        cost_estimate=pl.CostEstimate(
            flops=8 * rows * wide, bytes_accessed=12 * rows * wide, transcendentals=0
        ),
        name="finish",
    )(own, cot, weight, *backs, *events)


def tile_of(size, most):
    best = 128
    for tile in range(128, most + 1, 128):
        if size % tile == 0:
            best = tile
    return best


def slope_kernel(groups, index_ref, *refs):
    del index_ref
    pre_refs, sketch_ref = refs[:groups], refs[groups]
    slope_ref, down_ref = refs[-2:]
    pre = jnp.concatenate([r[0, 0, 0] for r in pre_refs], axis=0).astype(jnp.float32)
    sig = 0.5 + 0.5 * jnp.tanh(0.5 * pre)
    hidden = pre * sig
    slope = sig + hidden * (1.0 - sig)
    slope_ref[...] = slope.T.astype(slope_ref.dtype)
    term = lax.dot_general(
        hidden.astype(jnp.bfloat16), sketch_ref[...], NT, preferred_element_type=jnp.float32
    )

    @pl.when(pl.program_id(0) == 0)
    def _():
        down_ref[...] = jnp.zeros_like(down_ref)

    down_ref[...] += term


def slopes(chunk, pre, sketch_t, place, core, *events):
    n, _, _, rows, cols = pre.shape
    rank = sketch_t.shape[0]
    groups = 2 * n
    tile = tile_of(cols, 896)
    index = jnp.stack([place, core]).astype(jnp.int32)

    def spec_of(h, slot):
        return pl.BlockSpec(
            (1, 1, 1, rows, tile), lambda j, ix: (ix[0] ^ slot, ix[1] ^ h, chunk, 0, j)
        )

    return pl.pallas_call(
        functools.partial(slope_kernel, groups),
        grid_spec=pltpu.PrefetchScalarGridSpec(
            num_scalar_prefetch=1,
            grid=(cols // tile,),
            in_specs=[spec_of(h, slot) for h in range(2) for slot in range(n)]
            + [pl.BlockSpec((rank, tile), lambda j, ix: (0, j))]
            + [ANYWHERE] * len(events),
            out_specs=[
                pl.BlockSpec((tile, groups * rows), lambda j, ix: (j, 0)),
                pl.BlockSpec((groups * rows, rank), lambda j, ix: (0, 0)),
            ],
        ),
        out_shape=[
            jax.ShapeDtypeStruct((cols, groups * rows), jnp.bfloat16),
            jax.ShapeDtypeStruct((groups * rows, rank), jnp.float32),
        ],
        cost_estimate=pl.CostEstimate(
            flops=2 * groups * rows * cols * rank,
            bytes_accessed=4 * groups * rows * cols,
            transcendentals=groups * rows * cols,
        ),
        compiler_params=pltpu.CompilerParams(vmem_limit_bytes=7 << 20),
        name="slopes",
    )(index, *([pre] * groups), sketch_t, *events)


def expert_kernel(
    tile_f, tile_d, rows_ref, slope_ref, down_part_ref, sketch_ref, down_hbm, up_hbm, *refs
):
    keep_ref, give_ref, rows_buf, grad_buf, down_buf, up_buf, down_sem, up_sem = refs[-8:]
    hidden_cols, width = down_buf.shape
    steps_f, steps_d = hidden_cols // tile_f, width // tile_d
    half = keep_ref.shape[0]

    def tile(j, size):
        return pl.ds(pl.multiple_of(j * size, size), size)

    def down_copy(j):
        part = tile(j, tile_f)
        return pltpu.make_async_copy(down_hbm.at[part], down_buf.at[part], down_sem.at[j])

    def up_copy(j):
        part = tile(j, tile_d)
        return pltpu.make_async_copy(up_hbm.at[part], up_buf.at[part], up_sem.at[j])

    for j in range(min(AHEAD, steps_f)):
        down_copy(j).start()
    rows_buf[...] = rows_ref[...].T

    def first(j, carry):
        down_copy(j).wait()

        @pl.when(j + AHEAD < steps_f)
        def _():
            down_copy(j + AHEAD).start()

        @pl.when(j + AHEAD >= steps_f)
        def _():
            up_copy(j + AHEAD - steps_f).start()

        part = tile(j, tile_f)
        grad_hidden = jnp.dot(
            down_buf[part, :], rows_buf[...], preferred_element_type=jnp.float32
        )
        slope = slope_ref[part, :].astype(jnp.float32)
        grad_buf[part, :] = (grad_hidden * slope).astype(jnp.bfloat16)
        return carry

    lax.fori_loop(0, steps_f, first, 0)

    up_part = jnp.dot(sketch_ref[...], grad_buf[...], preferred_element_type=jnp.float32).T
    vectors = jnp.concatenate([down_part_ref[...], up_part], axis=1)
    keep_ref[:, width:] = vectors[:half]
    give_ref[:, width:] = vectors[half:].astype(jnp.bfloat16)

    def second(j, carry):
        up_copy(j).wait()

        @pl.when(j + AHEAD < steps_d)
        def _():
            up_copy(j + AHEAD).start()

        part = tile(j, tile_d)
        term = jnp.dot(up_buf[part, :], grad_buf[...], preferred_element_type=jnp.float32).T
        keep_ref[:, part] = term[:half]
        give_ref[:, part] = term[half:].astype(jnp.bfloat16)
        return carry

    lax.fori_loop(0, steps_d, second, 0)


def expert(rows, slope, down_part, sketch_t, down_local, up_local, *events):
    count, width = rows.shape
    hidden_cols = down_local.shape[0]
    rank = sketch_t.shape[0]
    wide = width + 2 * rank
    tile_f, tile_d = tile_of(hidden_cols, 512), tile_of(width, 512)
    return pl.pallas_call(
        functools.partial(expert_kernel, tile_f, tile_d),
        in_specs=[RESIDENT] * 4 + [ANYWHERE] * (2 + len(events)),
        out_specs=[RESIDENT] * 2,
        out_shape=[
            jax.ShapeDtypeStruct((count // 2, wide), jnp.float32),
            jax.ShapeDtypeStruct((count // 2, wide), jnp.bfloat16),
        ],
        scratch_shapes=[
            pltpu.VMEM((width, count), jnp.bfloat16),
            pltpu.VMEM((hidden_cols, count), jnp.bfloat16),
            pltpu.VMEM((hidden_cols, width), jnp.bfloat16),
            pltpu.VMEM((width, hidden_cols), jnp.bfloat16),
            pltpu.SemaphoreType.DMA((hidden_cols // tile_f,)),
            pltpu.SemaphoreType.DMA((width // tile_d,)),
        ],
        compiler_params=pltpu.CompilerParams(vmem_limit_bytes=38 << 20),
        cost_estimate=pl.CostEstimate(
            flops=4 * count * hidden_cols * width,
            bytes_accessed=4 * hidden_cols * width,
            transcendentals=0,
        ),
        name="expert",
    )(rows, slope, down_part, sketch_t, down_local, up_local, *events)


def per_device(
    cotangent,
    routes,
    gate_values,
    up_weight,
    down_weight,
    pre_activation,
    input_sketch,
    model_sketch,
    hidden_sketch,
    lengths,
):
    pieces = lax.axis_size("dp")
    sections = lax.axis_size("section")
    per_expert = pieces // EXPERTS
    place = lax.axis_index("dp")
    core = lax.axis_index("tensor")
    cot = cotangent[0]
    tok_dev, width = cot.shape
    half = tok_dev // 2
    rows = half // CHUNKS
    rank = model_sketch.shape[2]
    blocks = routes.shape[1]
    block_len = tok_dev // blocks
    sketch_local = hidden_sketch[0, 0]
    pre_all = pre_activation[0, 0]
    hidden_cols = pre_all.shape[2]
    pre_all = pre_all.reshape(pieces, 2, CHUNKS, rows, hidden_cols)

    def below(block):
        return lax.ppermute(block, "section", [(s, (s - 1) % sections) for s in range(sections)])

    token_routes = jnp.broadcast_to(routes[0][:, None, :], (blocks, block_len, 2)).reshape(
        tok_dev, 2
    )
    half_routes = lax.dynamic_slice_in_dim(token_routes, core * half, half, 0)
    half_gates = lax.dynamic_slice_in_dim(gate_values[0], core * half, half, 0)
    slot_expert = (place ^ jnp.arange(pieces, dtype=jnp.int32)) // per_expert
    hits = half_routes[:, None, :] == slot_expert[None, :, None]
    weight = jnp.sum(jnp.where(hits, half_gates[:, None, :], 0.0), axis=2)

    sketch_t = sketch_local.T
    cot_mine = lax.dynamic_slice_in_dim(cot, core * half, half, 0)
    cot_theirs = lax.dynamic_slice_in_dim(cot, (1 - core) * half, half, 0)
    order = sorted(range(1, pieces), key=lambda k: (bin(k).count("1"), -k))
    mark, keep, sent, grad, passed = (), (), (), (), ()
    below_mine, vectors = [], []
    for a in range(CHUNKS):
        part = slice(a * rows, (a + 1) * rows)
        mine, theirs = {0: cot_mine[part]}, {0: cot_theirs[part]}
        if mark:
            mine[0] = held(mine[0], *mark)
        for slot in order:
            low = slot & -slot
            mine[slot] = xored(mine[slot ^ low], "dp", low)
        slope, down_part = slopes(a, pre_all, sketch_t, place, core, *mark)
        mark = (mine[order[0]],)
        for level in range(1, pieces.bit_length()):
            slots = [k for k in order if bin(k).count("1") == level]
            if level > 1 and keep:
                for k in slots:
                    mine[k] = held(mine[k], *keep)
            traded = xored(jnp.concatenate([mine[k] for k in slots], axis=0), "tensor", 1)
            for at, slot in enumerate(slots):
                theirs[slot] = traded[at * rows : (at + 1) * rows]
        rows_in = jnp.concatenate(
            [mine[k] for k in range(pieces)] + [theirs[k] for k in range(pieces)], axis=0
        )

        kept, give = expert(
            rows_in, slope, down_part, sketch_t, down_weight[0, 0], up_weight[0, 0], *sent
        )
        keep = (kept,)
        if grad:
            give = held(give, *backs)
        own, *sent = merged(kept, xored(give, "tensor", 1), rows)
        backs = [xored(out, "dp", slot + 1) for slot, out in enumerate(sent)]
        if grad:
            passed = (below(held(*grad, backs[0])),)
            below_mine.append(*passed)
        new, vec = finished(own, cot_mine[part], weight[part], backs, *passed)
        grad = (new,)
        vectors.append(vec)
    below_mine.append(below(*grad))

    mine = jnp.concatenate(below_mine, axis=0)
    theirs = jnp.concatenate([xored(f, "tensor", 1) for f in below_mine], axis=0)
    handed = jnp.concatenate(
        [jnp.where(core == 0, mine, theirs), jnp.where(core == 0, theirs, mine)], axis=0
    )

    vec_mine = jnp.concatenate(vectors, axis=0)
    vec_theirs = xored(vec_mine, "tensor", 1)
    sketch_sum = jnp.concatenate(
        [jnp.where(core == 0, vec_mine, vec_theirs), jnp.where(core == 0, vec_theirs, vec_mine)],
        axis=0,
    )
    out_vec = jnp.dot(cot, model_sketch[0], preferred_element_type=jnp.float32)
    counts = lengths[0, 0]
    upto = jnp.arange(counts.shape[0])
    ends = jnp.sum(jnp.where(upto[None, :] <= upto[:, None], counts[None, :], 0), axis=1)
    starts = ends - counts
    position = jnp.arange(tok_dev, dtype=jnp.int32)
    member = ((position[None, :] >= starts[:, None]) & (position[None, :] < ends[:, None])).astype(
        jnp.float32
    )
    down_feat = jnp.einsum(
        "et,ta,tb->eab", member, out_vec, sketch_sum[:, :rank], precision=lax.Precision.HIGHEST
    )
    up_feat = jnp.einsum(
        "et,ta,tb->eab",
        member,
        sketch_sum[:, rank:],
        input_sketch[0],
        precision=lax.Precision.HIGHEST,
    )
    features = jnp.concatenate([down_feat, up_feat], axis=2)
    return (handed[None], features[None])


def solution(mesh):
    in_specs = (
        P("section", ("groups", "dp"), None),
        P("section", ("groups", "dp"), None),
        P("section", ("groups", "dp"), None),
        P("section", "dp", None, "tensor"),
        P("section", "dp", "tensor", None),
        P("section", ("groups", "dp"), None, None, "tensor"),
        P("section", ("groups", "dp"), None),
        P("section", None, None),
        P("section", "dp", "tensor", None),
        P("section", ("groups", "dp"), None),
    )
    out_specs = (P("section", ("groups", "dp"), None), P("section", ("groups", "dp"), None, None))
    return jax.shard_map(
        per_device, mesh=mesh, in_specs=in_specs, out_specs=out_specs, check_vma=False
    )
```

profile of v0, /device:TPU:0, one launch (start us, length us, event | category | flops | bytes accessed | tf_op | source)
XLA Modules:
  0.0 86.2 jit_solution(12228284083235916342)
XLA Ops:
  0.7 1.0 %constant_dynamic-update-slice_fusion.4 = (bf16[256,2048]{1,0:T(8,128)(2,1)S(1)}, bf16[32,2048]{1,0:T(8,128)(2,1)S(1)}) fusion(bf16[1,128,2048]{2,1,0:T(8,128)(2,1)} %param.10, s32[]{:T(128)S(6)} %select_n.45), kind=kLoop, calls=%fused_computation.37 | loop fusion | bytes 393220
  1.6 3.1 %collective-permute-start = (bf16[32,2048]{1,0:T(8,128)(2,1)S(1)}, bf16[32,2048]{1,0:T(8,128)(2,1)S(1)}, u32[]{:S(2)}, u32[]{:S(2)}) collective-permute-start(bf16[32,2048]{1,0:T(8,128)(2,1)S(1)} %get-tuple-element.43.cot_ref), channel_id=1, source_target_pairs={{0,4},{4,0},{8,12},{12,8},{1,5},{5,1},{9,13},{13,9},{2,6},{6,2},{1... | collective-permute-start | bytes 393224 | tf_op jit(solution)/shard_map/ppermute | solution.py:18
  4.7 2.6 %collective-permute-start.1 = (bf16[32,2048]{1,0:T(8,128)(2,1)S(1)}, bf16[32,2048]{1,0:T(8,128)(2,1)S(1)}, u32[]{:S(2)}, u32[]{:S(2)}) collective-permute-start(bf16[32,2048]{1,0:T(8,128)(2,1)S(1)} %get-tuple-element.43.cot_ref), channel_id=1, source_target_pairs={{0,8},{4,12},{8,0},{12,4},{1,9},{5,13},{9,1},{13,5},{2,10},{6,14},... | collective-permute-start | bytes 393224 | tf_op jit(solution)/shard_map/ppermute | solution.py:18
  7.3 0.9 %dynamic-slice_bitcast_fusion.1.block_ref.cot_ref = bf16[32,2048]{1,0:T(8,128)(2,1)S(1)} fusion(bf16[1,128,2048]{2,1,0:T(8,128)(2,1)} %param.10, s32[]{:T(128)S(6)} %add.13), kind=kLoop, calls=%fused_computation.14 | loop fusion | bytes 262148 | tf_op jit(solution)/shard_map/slice | solution.py:308
  9.1 2.0 %copy-done.1 = bf16[1,1,4,128,3584]{4,3,2,1,0:T(8,128)(2,1)S(1)} copy-done((bf16[1,1,4,128,3584]{4,3,2,1,0:T(8,128)(2,1)S(1)}, bf16[1,1,4,128,3584]{4,3,2,1,0:T(8,128)(2,1)}, u32[]{:S(2)}) %copy-start.1) | copy-done | bytes 3670040
  11.1 1.0 %copy-done.3 = bf16[1,1,3584,64]{2,3,1,0:T(8,128)(2,1)S(1)} copy-done((bf16[1,1,3584,64]{2,3,1,0:T(8,128)(2,1)S(1)}, bf16[1,1,3584,64]{2,3,1,0:T(8,128)(2,1)}, u32[]{:S(2)}) %copy-start.3) | copy-done | bytes 458776
  12.1 3.0 %slopes.2 = (bf16[3584,256]{1,0:T(8,128)(2,1)S(1)}, f32[256,64]{1,0:T(8,128)S(1)}) custom-call(s32[2]{0:T(128)S(1)} %pad_add_fusion.index_ref, bf16[4,2,2,32,3584]{4,3,2,1,0:T(8,128)(2,1)S(1)} %bitcast.49, bf16[4,2,2,32,3584]{4,3,2,1,0:T(8,128)(2,1)S(1)} %bitcast.50, bf16[4,2,2,32,3584]{4,3,2,1,0:T(8,128)(2,1)S(1)} %bitcast.51, ...), custom_call_target="tpu_custom_call" | custom-call | flops 117440512 | bytes 3670016 | tf_op jit(solution)/shard_map/slopes/pallas_call | solution.py:135
  16.7 1.2 %collective-permute-start.2 = (bf16[32,2048]{1,0:T(8,128)(2,1)S(1)}, bf16[32,2048]{1,0:T(8,128)(2,1)S(1)}, u32[]{:S(2)}, u32[]{:S(2)}) collective-permute-start(bf16[32,2048]{1,0:T(8,128)(2,1)S(1)} %collective-permute-done.1.refs_0_.refs_9_), channel_id=1, source_target_pairs={{0,4},{4,0},{8,12},{12,8},{1,5},{5,1},{9,13},{13,9},{2,6},{6,2},{1... | collective-permute-start | bytes 393224 | tf_op jit(solution)/shard_map/ppermute | solution.py:18
  17.9 3.0 %slopes.3 = (bf16[3584,256]{1,0:T(8,128)(2,1)S(1)}, f32[256,64]{1,0:T(8,128)S(1)}) custom-call(s32[2]{0:T(128)S(1)} %pad_add_fusion.index_ref, bf16[4,2,2,32,3584]{4,3,2,1,0:T(8,128)(2,1)S(1)} %bitcast.57, bf16[4,2,2,32,3584]{4,3,2,1,0:T(8,128)(2,1)S(1)} %bitcast.58, bf16[4,2,2,32,3584]{4,3,2,1,0:T(8,128)(2,1)S(1)} %bitcast.59, ...), custom_call_target="tpu_custom_call" | custom-call | flops 117440512 | bytes 3670016 | tf_op jit(solution)/shard_map/slopes/pallas_call | solution.py:135
  21.0 5.2 %collective-permute-done.2 = bf16[32,2048]{1,0:T(8,128)(2,1)S(1)} collective-permute-done((bf16[32,2048]{1,0:T(8,128)(2,1)S(1)}, bf16[32,2048]{1,0:T(8,128)(2,1)S(1)}, u32[]{:S(2)}, u32[]{:S(2)}) %collective-permute-start.2) | collective-permute-done | bytes 131104 | tf_op jit(solution)/shard_map/ppermute | solution.py:18
  26.9 1.1 %collective-permute-done.4 = bf16[32,2048]{1,0:T(8,128)(2,1)S(1)} collective-permute-done((bf16[32,2048]{1,0:T(8,128)(2,1)S(1)}, bf16[32,2048]{1,0:T(8,128)(2,1)S(1)}, u32[]{:S(2)}, u32[]{:S(2)}) %collective-permute-start.4) | collective-permute-done | bytes 131104 | tf_op jit(solution)/shard_map/ppermute | solution.py:18
  28.1 13.4 %expert.2 = (f32[128,2176]{1,0:T(8,128)S(1)}, bf16[128,2176]{1,0:T(8,128)(2,1)S(1)}) custom-call(bf16[256,2048]{1,0:T(8,128)(2,1)S(1)} %constant_dynamic-update-slice_fusion.rows_ref, bf16[3584,256]{1,0:T(8,128)(2,1)S(1)} %get-tuple-element.22.slope_ref, f32[256,64]{1,0:T(8,128)S(1)} %get-tuple-element.23.down_part_ref, bf16[64,3584]{1,0:T(8,128)(2,1)S(1)} %bitcast.67, ...), custom_call_target="tpu_custom_call" | custom-call | flops 7516192768 | bytes 29360128 | tf_op jit(solution)/shard_map/expert/pallas_call | solution.py:233
  43.8 1.0 %collective-permute-start.6 = (bf16[32,2176]{1,0:T(8,128)(2,1)S(1)}, bf16[32,2176]{1,0:T(8,128)(2,1)S(1)}, u32[]{:S(2)}, u32[]{:S(2)}) collective-permute-start(bf16[32,2176]{1,0:T(8,128)(2,1)S(1)} %get-tuple-element.27.refs_0_), channel_id=1, source_target_pairs={{0,4},{4,0},{8,12},{12,8},{1,5},{5,1},{9,13},{13,9},{2,6},{6,2},{1... | collective-permute-start | bytes 417800 | tf_op jit(solution)/shard_map/ppermute | solution.py:18
  45.6 2.7 %collective-permute-start.8 = (bf16[32,2176]{1,0:T(8,128)(2,1)S(1)}, bf16[32,2176]{1,0:T(8,128)(2,1)S(1)}, u32[]{:S(2)}, u32[]{:S(2)}) collective-permute-start(bf16[32,2176]{1,0:T(8,128)(2,1)S(1)} %get-tuple-element.29.refs_2_), channel_id=1, source_target_pairs={{0,12},{4,8},{8,4},{12,0},{1,13},{5,9},{9,5},{13,1},{2,14},{6,10},... | collective-permute-start | bytes 417800 | tf_op jit(solution)/shard_map/ppermute | solution.py:18
  48.3 13.4 %expert.3 = (f32[128,2176]{1,0:T(8,128)S(1)}, bf16[128,2176]{1,0:T(8,128)(2,1)S(1)}) custom-call(bf16[256,2048]{1,0:T(8,128)(2,1)S(1)} %constant_dynamic-update-slice_fusion.5.rows_ref, bf16[3584,256]{1,0:T(8,128)(2,1)S(1)} %get-tuple-element.31.slope_ref, f32[256,64]{1,0:T(8,128)S(1)} %get-tuple-element.32.down_part_ref, bf16[64,3584]{1,0:T(8,128)(2,1)S(1)} %bitcast.68, ...), custom_call_target="tpu_custom_call" | custom-call | flops 7516192768 | bytes 29360128 | tf_op jit(solution)/shard_map/expert/pallas_call | solution.py:233
  62.1 1.3 %fusion = f32[128,64]{0,1:T(8,128)S(1)} fusion(bf16[1,128,2048]{2,1,0:T(8,128)(2,1)} %param.10, bf16[1,2048,64]{1,2,0:T(8,128)(2,1)S(1)} %copy-done), kind=kOutput, calls=%fused_computation.3 | convolution fusion | flops 33554432 | bytes 819200 | tf_op jit(solution)/shard_map/dot_general | solution.py:356
  64.2 1.8 %collective-permute-start.17 = (bf16[32,2176]{1,0:T(8,128)(2,1)S(1)}, bf16[32,2176]{1,0:T(8,128)(2,1)S(1)}, u32[]{:S(2)}, u32[]{:S(2)}) collective-permute-start(bf16[32,2176]{1,0:T(8,128)(2,1)S(1)} %get-tuple-element.37), channel_id=1, source_target_pairs={{0,8},{4,12},{8,0},{12,4},{1,9},{5,13},{9,1},{13,5},{2,10},{6,14},... | collective-permute-start | bytes 417800 | tf_op jit(solution)/shard_map/ppermute | solution.py:18
  66.0 2.7 %collective-permute-start.18 = (bf16[32,2176]{1,0:T(8,128)(2,1)S(1)}, bf16[32,2176]{1,0:T(8,128)(2,1)S(1)}, u32[]{:S(2)}, u32[]{:S(2)}) collective-permute-start(bf16[32,2176]{1,0:T(8,128)(2,1)S(1)} %get-tuple-element.38), channel_id=1, source_target_pairs={{0,12},{4,8},{8,4},{12,0},{1,13},{5,9},{9,5},{13,1},{2,14},{6,10},... | collective-permute-start | bytes 417800 | tf_op jit(solution)/shard_map/ppermute | solution.py:18
  68.7 2.4 %collective-permute-done.15.refs_0_ = bf16[32,2176]{1,0:T(8,128)(2,1)S(1)} collective-permute-done((bf16[32,2176]{1,0:T(8,128)(2,1)S(1)}, bf16[32,2176]{1,0:T(8,128)(2,1)S(1)}, u32[]{:S(2)}, u32[]{:S(2)}) %collective-permute-start.15) | collective-permute-done | bytes 139296 | tf_op jit(solution)/shard_map/ppermute | solution.py:18
  71.1 1.6 %collective-permute-start.16 = (bf16[32,2048]{1,0:T(8,128)(2,1)S(1)}, bf16[32,2048]{1,0:T(8,128)(2,1)S(1)}, u32[]{:S(2)}, u32[]{:S(2)}) collective-permute-start(bf16[32,2048]{1,0:T(8,128)(2,1)S(1)} %held.7), channel_id=1, source_target_pairs={{0,2},{2,0},{1,3},{3,1},{4,6},{6,4},{5,7},{7,5},{8,10},{10,8},{9,1... | collective-permute-start | bytes 393224 | tf_op jit(solution)/shard_map/ppermute | solution.py:289
  72.8 4.9 %collective-permute-done.17.refs_1_ = bf16[32,2176]{1,0:T(8,128)(2,1)S(1)} collective-permute-done((bf16[32,2176]{1,0:T(8,128)(2,1)S(1)}, bf16[32,2176]{1,0:T(8,128)(2,1)S(1)}, u32[]{:S(2)}, u32[]{:S(2)}) %collective-permute-start.17) | collective-permute-done | bytes 139296 | tf_op jit(solution)/shard_map/ppermute | solution.py:18
  78.0 1.6 %collective-permute-start.19 = (bf16[32,2048]{1,0:T(8,128)(2,1)S(1)}, bf16[32,2048]{1,0:T(8,128)(2,1)S(1)}, u32[]{:S(2)}, u32[]{:S(2)}) collective-permute-start(bf16[32,2048]{1,0:T(8,128)(2,1)S(1)} %get-tuple-element.39), channel_id=1, source_target_pairs={{0,2},{2,0},{1,3},{3,1},{4,6},{6,4},{5,7},{7,5},{8,10},{10,8},{9,1... | collective-permute-start | bytes 393224 | tf_op jit(solution)/shard_map/ppermute | solution.py:289
  81.3 2.7 %collective-permute-done.19 = bf16[32,2048]{1,0:T(8,128)(2,1)S(1)} collective-permute-done((bf16[32,2048]{1,0:T(8,128)(2,1)S(1)}, bf16[32,2048]{1,0:T(8,128)(2,1)S(1)}, u32[]{:S(2)}, u32[]{:S(2)}) %collective-permute-start.19) | collective-permute-done | bytes 131104 | tf_op jit(solution)/shard_map/ppermute | solution.py:289
  84.0 1.3 %collective-permute-done.21 = bf16[32,2048]{1,0:T(8,128)(2,1)S(1)} collective-permute-done((bf16[32,2048]{1,0:T(8,128)(2,1)S(1)}, bf16[32,2048]{1,0:T(8,128)(2,1)S(1)}, u32[]{:S(2)}, u32[]{:S(2)}) %collective-permute-start.21) | collective-permute-done | bytes 131104 | tf_op jit(solution)/shard_map/ppermute | solution.py:18
  (96 shorter events, 10.3 us)
Async XLA Ops:
  0.6 61.5 %copy-start = (bf16[1,2048,64]{1,2,0:T(8,128)(2,1)S(1)}, bf16[1,2048,64]{1,2,0:T(8,128)(2,1)}, u32[]{:S(2)}) copy-start(bf16[1,2048,64]{1,2,0:T(8,128)(2,1)} %param.17) | copy-start | bytes 786436
  1.6 14.9 %collective-permute-start = (bf16[32,2048]{1,0:T(8,128)(2,1)S(1)}, bf16[32,2048]{1,0:T(8,128)(2,1)S(1)}, u32[]{:S(2)}, u32[]{:S(2)}) collective-permute-start(bf16[32,2048]{1,0:T(8,128)(2,1)S(1)} %get-tuple-element.43.cot_ref), channel_id=1, source_target_pairs={{0,4},{4,0},{8,12},{12,8},{1,5},{5,1},{9,13},{13,9},{2,6},{6,2},{1... | collective-permute-start | bytes 393224 | tf_op jit(solution)/shard_map/ppermute | solution.py:18
  4.7 10.5 %collective-permute-start.1 = (bf16[32,2048]{1,0:T(8,128)(2,1)S(1)}, bf16[32,2048]{1,0:T(8,128)(2,1)S(1)}, u32[]{:S(2)}, u32[]{:S(2)}) collective-permute-start(bf16[32,2048]{1,0:T(8,128)(2,1)S(1)} %get-tuple-element.43.cot_ref), channel_id=1, source_target_pairs={{0,8},{4,12},{8,0},{12,4},{1,9},{5,13},{9,1},{13,5},{2,10},{6,14},... | collective-permute-start | bytes 393224 | tf_op jit(solution)/shard_map/ppermute | solution.py:18
  15.3 10.9 %collective-permute-start.10 = (bf16[32,2048]{1,0:T(8,128)(2,1)S(1)}, bf16[32,2048]{1,0:T(8,128)(2,1)S(1)}, u32[]{:S(2)}, u32[]{:S(2)}) collective-permute-start(bf16[32,2048]{1,0:T(8,128)(2,1)S(1)} %held.4), channel_id=1, source_target_pairs={{0,8},{4,12},{8,0},{12,4},{1,9},{5,13},{9,1},{13,5},{2,10},{6,14},... | collective-permute-start | bytes 393224 | tf_op jit(solution)/shard_map/ppermute | solution.py:18
  15.7 10.6 %collective-permute-start.9 = (bf16[32,2048]{1,0:T(8,128)(2,1)S(1)}, bf16[32,2048]{1,0:T(8,128)(2,1)S(1)}, u32[]{:S(2)}, u32[]{:S(2)}) collective-permute-start(bf16[32,2048]{1,0:T(8,128)(2,1)S(1)} %held.4), channel_id=1, source_target_pairs={{0,4},{4,0},{8,12},{12,8},{1,5},{5,1},{9,13},{13,9},{2,6},{6,2},{1... | collective-permute-start | bytes 393224 | tf_op jit(solution)/shard_map/ppermute | solution.py:18
  16.6 10.3 %collective-permute-start.3 = (bf16[64,2048]{1,0:T(8,128)(2,1)S(1)}, bf16[64,2048]{1,0:T(8,128)(2,1)S(1)}, u32[]{:S(2)}, u32[]{:S(2)}) collective-permute-start(bf16[64,2048]{1,0:T(8,128)(2,1)S(1)} %pad_maximum_fusion), channel_id=1, source_target_pairs={{0,1},{1,0},{2,3},{3,2},{4,5},{5,4},{6,7},{7,6},{8,9},{9,8},{10,11... | collective-permute-start | bytes 786440 | tf_op jit(solution)/shard_map/ppermute | solution.py:18
  16.7 9.5 %collective-permute-start.2 = (bf16[32,2048]{1,0:T(8,128)(2,1)S(1)}, bf16[32,2048]{1,0:T(8,128)(2,1)S(1)}, u32[]{:S(2)}, u32[]{:S(2)}) collective-permute-start(bf16[32,2048]{1,0:T(8,128)(2,1)S(1)} %collective-permute-done.1.refs_0_.refs_9_), channel_id=1, source_target_pairs={{0,4},{4,0},{8,12},{12,8},{1,5},{5,1},{9,13},{13,9},{2,6},{6,2},{1... | collective-permute-start | bytes 393224 | tf_op jit(solution)/shard_map/ppermute | solution.py:18
  26.2 15.9 %collective-permute-start.12 = (bf16[64,2048]{1,0:T(8,128)(2,1)S(1)}, bf16[64,2048]{1,0:T(8,128)(2,1)S(1)}, u32[]{:S(2)}, u32[]{:S(2)}) collective-permute-start(bf16[64,2048]{1,0:T(8,128)(2,1)S(1)} %pad_maximum_fusion.1), channel_id=1, source_target_pairs={{0,1},{1,0},{2,3},{3,2},{4,5},{5,4},{6,7},{7,6},{8,9},{9,8},{10,11... | collective-permute-start | bytes 786440 | tf_op jit(solution)/shard_map/ppermute | solution.py:18
  26.3 1.7 %collective-permute-start.4 = (bf16[32,2048]{1,0:T(8,128)(2,1)S(1)}, bf16[32,2048]{1,0:T(8,128)(2,1)S(1)}, u32[]{:S(2)}, u32[]{:S(2)}) collective-permute-start(bf16[32,2048]{1,0:T(8,128)(2,1)S(1)} %collective-permute-done.2), channel_id=1, source_target_pairs={{0,1},{1,0},{2,3},{3,2},{4,5},{5,4},{6,7},{7,6},{8,9},{9,8},{10,11... | collective-permute-start | bytes 393224 | tf_op jit(solution)/shard_map/ppermute | solution.py:18
  26.8 14.6 %collective-permute-start.11 = (bf16[32,2048]{1,0:T(8,128)(2,1)S(1)}, bf16[32,2048]{1,0:T(8,128)(2,1)S(1)}, u32[]{:S(2)}, u32[]{:S(2)}) collective-permute-start(bf16[32,2048]{1,0:T(8,128)(2,1)S(1)} %collective-permute-done.10), channel_id=1, source_target_pairs={{0,4},{4,0},{8,12},{12,8},{1,5},{5,1},{9,13},{13,9},{2,6},{6,2},{1... | collective-permute-start | bytes 393224 | tf_op jit(solution)/shard_map/ppermute | solution.py:18
  41.5 1.4 %collective-permute-start.13 = (bf16[32,2048]{1,0:T(8,128)(2,1)S(1)}, bf16[32,2048]{1,0:T(8,128)(2,1)S(1)}, u32[]{:S(2)}, u32[]{:S(2)}) collective-permute-start(bf16[32,2048]{1,0:T(8,128)(2,1)S(1)} %held.5), channel_id=1, source_target_pairs={{0,1},{1,0},{2,3},{3,2},{4,5},{5,4},{6,7},{7,6},{8,9},{9,8},{10,11... | collective-permute-start | bytes 393224 | tf_op jit(solution)/shard_map/ppermute | solution.py:18
  41.7 2.0 %collective-permute-start.5 = (bf16[128,2176]{1,0:T(8,128)(2,1)S(1)}, bf16[128,2176]{1,0:T(8,128)(2,1)S(1)}, u32[]{:S(2)}, u32[]{:S(2)}) collective-permute-start(bf16[128,2176]{1,0:T(8,128)(2,1)S(1)} %get-tuple-element.25), channel_id=1, source_target_pairs={{0,1},{1,0},{2,3},{3,2},{4,5},{5,4},{6,7},{7,6},{8,9},{9,8},{10,11... | collective-permute-start | bytes 1671176 | tf_op jit(solution)/shard_map/ppermute | solution.py:18
  43.8 17.9 %collective-permute-start.6 = (bf16[32,2176]{1,0:T(8,128)(2,1)S(1)}, bf16[32,2176]{1,0:T(8,128)(2,1)S(1)}, u32[]{:S(2)}, u32[]{:S(2)}) collective-permute-start(bf16[32,2176]{1,0:T(8,128)(2,1)S(1)} %get-tuple-element.27.refs_0_), channel_id=1, source_target_pairs={{0,4},{4,0},{8,12},{12,8},{1,5},{5,1},{9,13},{13,9},{2,6},{6,2},{1... | collective-permute-start | bytes 417800 | tf_op jit(solution)/shard_map/ppermute | solution.py:18
  44.8 16.9 %collective-permute-start.7 = (bf16[32,2176]{1,0:T(8,128)(2,1)S(1)}, bf16[32,2176]{1,0:T(8,128)(2,1)S(1)}, u32[]{:S(2)}, u32[]{:S(2)}) collective-permute-start(bf16[32,2176]{1,0:T(8,128)(2,1)S(1)} %get-tuple-element.28.refs_1_), channel_id=1, source_target_pairs={{0,8},{4,12},{8,0},{12,4},{1,9},{5,13},{9,1},{13,5},{2,10},{6,14},... | collective-permute-start | bytes 417800 | tf_op jit(solution)/shard_map/ppermute | solution.py:18
  45.6 16.1 %collective-permute-start.8 = (bf16[32,2176]{1,0:T(8,128)(2,1)S(1)}, bf16[32,2176]{1,0:T(8,128)(2,1)S(1)}, u32[]{:S(2)}, u32[]{:S(2)}) collective-permute-start(bf16[32,2176]{1,0:T(8,128)(2,1)S(1)} %get-tuple-element.29.refs_2_), channel_id=1, source_target_pairs={{0,12},{4,8},{8,4},{12,0},{1,13},{5,9},{9,5},{13,1},{2,14},{6,10},... | collective-permute-start | bytes 417800 | tf_op jit(solution)/shard_map/ppermute | solution.py:18
  61.8 2.0 %collective-permute-start.14 = (bf16[128,2176]{1,0:T(8,128)(2,1)S(1)}, bf16[128,2176]{1,0:T(8,128)(2,1)S(1)}, u32[]{:S(2)}, u32[]{:S(2)}) collective-permute-start(bf16[128,2176]{1,0:T(8,128)(2,1)S(1)} %held.6), channel_id=1, source_target_pairs={{0,1},{1,0},{2,3},{3,2},{4,5},{5,4},{6,7},{7,6},{8,9},{9,8},{10,11... | collective-permute-start | bytes 1671176 | tf_op jit(solution)/shard_map/ppermute | solution.py:18
  64.0 7.1 %collective-permute-start.15 = (bf16[32,2176]{1,0:T(8,128)(2,1)S(1)}, bf16[32,2176]{1,0:T(8,128)(2,1)S(1)}, u32[]{:S(2)}, u32[]{:S(2)}) collective-permute-start(bf16[32,2176]{1,0:T(8,128)(2,1)S(1)} %get-tuple-element.35), channel_id=1, source_target_pairs={{0,4},{4,0},{8,12},{12,8},{1,5},{5,1},{9,13},{13,9},{2,6},{6,2},{1... | collective-permute-start | bytes 417800 | tf_op jit(solution)/shard_map/ppermute | solution.py:18
  64.2 13.5 %collective-permute-start.17 = (bf16[32,2176]{1,0:T(8,128)(2,1)S(1)}, bf16[32,2176]{1,0:T(8,128)(2,1)S(1)}, u32[]{:S(2)}, u32[]{:S(2)}) collective-permute-start(bf16[32,2176]{1,0:T(8,128)(2,1)S(1)} %get-tuple-element.37), channel_id=1, source_target_pairs={{0,8},{4,12},{8,0},{12,4},{1,9},{5,13},{9,1},{13,5},{2,10},{6,14},... | collective-permute-start | bytes 417800 | tf_op jit(solution)/shard_map/ppermute | solution.py:18
  66.0 11.7 %collective-permute-start.18 = (bf16[32,2176]{1,0:T(8,128)(2,1)S(1)}, bf16[32,2176]{1,0:T(8,128)(2,1)S(1)}, u32[]{:S(2)}, u32[]{:S(2)}) collective-permute-start(bf16[32,2176]{1,0:T(8,128)(2,1)S(1)} %get-tuple-element.38), channel_id=1, source_target_pairs={{0,12},{4,8},{8,4},{12,0},{1,13},{5,9},{9,5},{13,1},{2,14},{6,10},... | collective-permute-start | bytes 417800 | tf_op jit(solution)/shard_map/ppermute | solution.py:18
  71.1 6.6 %collective-permute-start.16 = (bf16[32,2048]{1,0:T(8,128)(2,1)S(1)}, bf16[32,2048]{1,0:T(8,128)(2,1)S(1)}, u32[]{:S(2)}, u32[]{:S(2)}) collective-permute-start(bf16[32,2048]{1,0:T(8,128)(2,1)S(1)} %held.7), channel_id=1, source_target_pairs={{0,2},{2,0},{1,3},{3,1},{4,6},{6,4},{5,7},{7,5},{8,10},{10,8},{9,1... | collective-permute-start | bytes 393224 | tf_op jit(solution)/shard_map/ppermute | solution.py:289
  77.9 1.8 %collective-permute-start.22 = (f32[64,128]{1,0:T(8,128)S(1)}, f32[64,128]{1,0:T(8,128)S(1)}, u32[]{:S(2)}, u32[]{:S(2)}) collective-permute-start(f32[64,128]{1,0:T(8,128)S(1)} %constant_dynamic-update-slice_fusion.14), channel_id=1, source_target_pairs={{0,1},{1,0},{2,3},{3,2},{4,5},{5,4},{6,7},{7,6},{8,9},{9,8},{10,11... | collective-permute-start | bytes 98312 | tf_op jit(solution)/shard_map/ppermute | solution.py:18
  78.0 5.9 %collective-permute-start.19 = (bf16[32,2048]{1,0:T(8,128)(2,1)S(1)}, bf16[32,2048]{1,0:T(8,128)(2,1)S(1)}, u32[]{:S(2)}, u32[]{:S(2)}) collective-permute-start(bf16[32,2048]{1,0:T(8,128)(2,1)S(1)} %get-tuple-element.39), channel_id=1, source_target_pairs={{0,2},{2,0},{1,3},{3,1},{4,6},{6,4},{5,7},{7,5},{8,10},{10,8},{9,1... | collective-permute-start | bytes 393224 | tf_op jit(solution)/shard_map/ppermute | solution.py:289
  79.6 4.4 %collective-permute-start.20 = (bf16[32,2048]{1,0:T(8,128)(2,1)S(1)}, bf16[32,2048]{1,0:T(8,128)(2,1)S(1)}, u32[]{:S(2)}, u32[]{:S(2)}) collective-permute-start(bf16[32,2048]{1,0:T(8,128)(2,1)S(1)} %collective-permute-done.16.refs_3_), channel_id=1, source_target_pairs={{0,1},{1,0},{2,3},{3,2},{4,5},{5,4},{6,7},{7,6},{8,9},{9,8},{10,11... | collective-permute-start | bytes 393224 | tf_op jit(solution)/shard_map/ppermute | solution.py:18
  83.9 1.3 %collective-permute-start.21 = (bf16[32,2048]{1,0:T(8,128)(2,1)S(1)}, bf16[32,2048]{1,0:T(8,128)(2,1)S(1)}, u32[]{:S(2)}, u32[]{:S(2)}) collective-permute-start(bf16[32,2048]{1,0:T(8,128)(2,1)S(1)} %collective-permute-done.19), channel_id=1, source_target_pairs={{0,1},{1,0},{2,3},{3,2},{4,5},{5,4},{6,7},{7,6},{8,9},{9,8},{10,11... | collective-permute-start | bytes 393224 | tf_op jit(solution)/shard_map/ppermute | solution.py:18
  (8 other events, 57.0 us)
where the time goes:
time: 86.6 us; the launch traced here: 86.2 us
  Pallas kernels  33.5 us (39%)
  starting transfers between devices  21.9 us (25%)
  waiting for transfers between devices  19.5 us (23%)
  local copies, waits for them, and re-layouts  6.27 us (7%)
  other arithmetic  2.12 us (2%)
  matrix products  1.86 us (2%)
  between operations  1.08 us (1%)
    pallas_call x2, Pallas kernels, expert(): pl.pallas_call(functools.partial(expert_kernel, tile_f, tile_d), in_specs...  26.8 us
    ppermute x21, starting transfers between devices, xored(): return lax.ppermute(block, axis, [(i, i ^ bits) for i in range(n)])  18.7 us
    ppermute x21, waiting for transfers between devices, xored(): return lax.ppermute(block, axis, [(i, i ^ bits) for i in range(n)])  16.8 us
    pallas_call x2, Pallas kernels, slopes(): pl.pallas_call(functools.partial(slope_kernel, groups), grid_spec=pltpu.P...  6.06 us
    unnamed x37, local copies, waits for them, and re-layouts  4.41 us
    ppermute x2, starting transfers between devices, below(): lax.ppermute(block, 'section', [(s, (s - 1) % sections) for s in range(se...  3.12 us
    ppermute x2, waiting for transfers between devices, below(): lax.ppermute(block, 'section', [(s, (s - 1) % sections) for s in range(se...  2.67 us
  transfers between devices with their start and end apart: 23, of which 9 were waited for; matrix products, arithmetic and copies ran while one was open for 6% of the time, Pallas kernels for 38%

commit v1 on v0

--- a/solution.py
+++ b/solution.py
@@ -229,7 +229,7 @@
     hidden_cols = down_local.shape[0]
     rank = sketch_t.shape[0]
     wide = width + 2 * rank
-    tile_f, tile_d = tile_of(hidden_cols, 512), tile_of(width, 512)
+    tile_f, tile_d = tile_of(hidden_cols, 896), tile_of(width, 512)
     return pl.pallas_call(
         functools.partial(expert_kernel, tile_f, tile_d),
         in_specs=[RESIDENT] * 4 + [ANYWHERE] * (2 + len(events)),
@@ -300,7 +300,7 @@
     sketch_t = sketch_local.T
     cot_mine = lax.dynamic_slice_in_dim(cot, core * half, half, 0)
     cot_theirs = lax.dynamic_slice_in_dim(cot, (1 - core) * half, half, 0)
-    order = sorted(range(1, pieces), key=lambda k: (bin(k).count("1"), -k))
+    order = sorted(range(1, pieces), reverse=True)
     mark, keep, sent, grad, passed = (), (), (), (), ()
     below_mine, vectors = [], []
     for a in range(CHUNKS):
@@ -309,18 +309,15 @@
         if mark:
             mine[0] = held(mine[0], *mark)
         for slot in order:
-            low = slot & -slot
-            mine[slot] = xored(mine[slot ^ low], "dp", low)
-        slope, down_part = slopes(a, pre_all, sketch_t, place, core, *mark)
-        mark = (mine[order[0]],)
-        for level in range(1, pieces.bit_length()):
-            slots = [k for k in order if bin(k).count("1") == level]
-            if level > 1 and keep:
-                for k in slots:
-                    mine[k] = held(mine[k], *keep)
-            traded = xored(jnp.concatenate([mine[k] for k in slots], axis=0), "tensor", 1)
-            for at, slot in enumerate(slots):
-                theirs[slot] = traded[at * rows : (at + 1) * rows]
+            mine[slot] = xored(mine[0], "dp", slot)
+        slope, down_part = slopes(a, pre_all, sketch_t, place, core)
+        mark = (mine[1],)
+        if keep:
+            for slot in order:
+                mine[slot] = held(mine[slot], *keep)
+        traded = xored(jnp.concatenate([mine[slot] for slot in order], axis=0), "tensor", 1)
+        for at, slot in enumerate(order):
+            theirs[slot] = traded[at * rows : (at + 1) * rows]
         rows_in = jnp.concatenate(
             [mine[k] for k in range(pieces)] + [theirs[k] for k in range(pieces)], axis=0
         )

time: 86.6 us -> 83.2 us (0.961)
  waiting for transfers between devices: 19.5 us -> 16.2 us
  Pallas kernels: 33.5 us -> 31.6 us
  starting transfers between devices: 21.9 us -> 23.5 us
    ppermute x21 -> x19, waiting for transfers between devices: 16.8 us -> 13.6 us  [xored(): return lax.ppermute(block, axis, [(i, i ^ bits) for i in range(n)])]
    pallas_call x2, Pallas kernels: 26.8 us -> 24.9 us  [expert(): pl.pallas_call(functools.partial(expert_kernel, tile_f, tile_d), in_specs...]
    ppermute x21 -> x19, starting transfers between devices: 18.7 us -> 20.1 us  [xored(): return lax.ppermute(block, axis, [(i, i ^ bits) for i in range(n)])]
    unnamed x37 -> x35, local copies, waits for them, and re-layouts: 4.41 us -> 4.42 us
  transfers between devices with their start and end apart: 23 -> 21, of which waited for: 9 -> 8; matrix products, arithmetic and copies ran while one was open for 6% -> 6% of each run, Pallas kernels for 38% -> 38%
where the time goes in v1:
time: 83.2 us; the launch traced here: 82.8 us
  Pallas kernels  31.6 us (38%)
  starting transfers between devices  23.5 us (28%)
  waiting for transfers between devices  16.2 us (19%)
  local copies, waits for them, and re-layouts  6.28 us (8%)
  other arithmetic  2.13 us (3%)
  matrix products  1.86 us (2%)
  between operations  1.1 us (1%)
    pallas_call x2, Pallas kernels, expert(): pl.pallas_call(functools.partial(expert_kernel, tile_f, tile_d), in_specs...  24.9 us
    ppermute x19, starting transfers between devices, xored(): return lax.ppermute(block, axis, [(i, i ^ bits) for i in range(n)])  20.1 us
    ppermute x19, waiting for transfers between devices, xored(): return lax.ppermute(block, axis, [(i, i ^ bits) for i in range(n)])  13.6 us
    pallas_call x2, Pallas kernels, slopes(): pl.pallas_call(functools.partial(slope_kernel, groups), grid_spec=pltpu.P...  6.07 us
    unnamed x35, local copies, waits for them, and re-layouts  4.42 us
    ppermute x2, starting transfers between devices, below(): lax.ppermute(block, 'section', [(s, (s - 1) % sections) for s in range(se...  3.41 us
    ppermute x2, waiting for transfers between devices, below(): lax.ppermute(block, 'section', [(s, (s - 1) % sections) for s in range(se...  2.67 us
  transfers between devices with their start and end apart: 21, of which 8 were waited for; matrix products, arithmetic and copies ran while one was open for 6% of the time, Pallas kernels for 38%

profile of v1, /device:TPU:0, one launch (start us, length us, event | category | flops | bytes accessed | tf_op | source)
XLA Modules:
  0.0 82.8 jit_solution(9488169711787215190)
XLA Ops:
  0.7 1.0 %constant_dynamic-update-slice_fusion.3 = (bf16[256,2048]{1,0:T(8,128)(2,1)S(1)}, bf16[32,2048]{1,0:T(8,128)(2,1)S(1)}) fusion(bf16[1,128,2048]{2,1,0:T(8,128)(2,1)} %param.10, s32[]{:T(128)S(6)} %select_n.45), kind=kLoop, calls=%fused_computation.38 | loop fusion | bytes 393220
  1.6 3.1 %collective-permute-start = (bf16[32,2048]{1,0:T(8,128)(2,1)S(1)}, bf16[32,2048]{1,0:T(8,128)(2,1)S(1)}, u32[]{:S(2)}, u32[]{:S(2)}) collective-permute-start(bf16[32,2048]{1,0:T(8,128)(2,1)S(1)} %get-tuple-element.43.cot_ref), channel_id=1, source_target_pairs={{0,4},{4,0},{8,12},{12,8},{1,5},{5,1},{9,13},{13,9},{2,6},{6,2},{1... | collective-permute-start | bytes 393224 | tf_op jit(solution)/shard_map/ppermute | solution.py:18
  4.7 2.6 %collective-permute-start.1 = (bf16[32,2048]{1,0:T(8,128)(2,1)S(1)}, bf16[32,2048]{1,0:T(8,128)(2,1)S(1)}, u32[]{:S(2)}, u32[]{:S(2)}) collective-permute-start(bf16[32,2048]{1,0:T(8,128)(2,1)S(1)} %get-tuple-element.43.cot_ref), channel_id=1, source_target_pairs={{0,8},{4,12},{8,0},{12,4},{1,9},{5,13},{9,1},{13,5},{2,10},{6,14},... | collective-permute-start | bytes 393224 | tf_op jit(solution)/shard_map/ppermute | solution.py:18
  7.3 0.9 %dynamic-slice_bitcast_fusion.1.block_ref.cot_ref = bf16[32,2048]{1,0:T(8,128)(2,1)S(1)} fusion(bf16[1,128,2048]{2,1,0:T(8,128)(2,1)} %param.10, s32[]{:T(128)S(6)} %add.13), kind=kLoop, calls=%fused_computation.15 | loop fusion | bytes 262148 | tf_op jit(solution)/shard_map/slice | solution.py:308
  9.1 2.0 %copy-done.1 = bf16[1,1,4,128,3584]{4,3,2,1,0:T(8,128)(2,1)S(1)} copy-done((bf16[1,1,4,128,3584]{4,3,2,1,0:T(8,128)(2,1)S(1)}, bf16[1,1,4,128,3584]{4,3,2,1,0:T(8,128)(2,1)}, u32[]{:S(2)}) %copy-start.1) | copy-done | bytes 3670040
  11.1 1.0 %copy-done.2 = bf16[1,1,3584,64]{2,3,1,0:T(8,128)(2,1)S(1)} copy-done((bf16[1,1,3584,64]{2,3,1,0:T(8,128)(2,1)S(1)}, bf16[1,1,3584,64]{2,3,1,0:T(8,128)(2,1)}, u32[]{:S(2)}) %copy-start.2) | copy-done | bytes 458776
  12.1 3.0 %slopes.2 = (bf16[3584,256]{1,0:T(8,128)(2,1)S(1)}, f32[256,64]{1,0:T(8,128)S(1)}) custom-call(s32[2]{0:T(128)S(1)} %pad_add_fusion.index_ref, bf16[4,2,2,32,3584]{4,3,2,1,0:T(8,128)(2,1)S(1)} %bitcast.49, bf16[4,2,2,32,3584]{4,3,2,1,0:T(8,128)(2,1)S(1)} %bitcast.50, bf16[4,2,2,32,3584]{4,3,2,1,0:T(8,128)(2,1)S(1)} %bitcast.51, ...), custom_call_target="tpu_custom_call" | custom-call | flops 117440512 | bytes 3670016 | tf_op jit(solution)/shard_map/slopes/pallas_call | solution.py:135
  15.2 3.0 %slopes.3 = (bf16[3584,256]{1,0:T(8,128)(2,1)S(1)}, f32[256,64]{1,0:T(8,128)S(1)}) custom-call(s32[2]{0:T(128)S(1)} %pad_add_fusion.index_ref, bf16[4,2,2,32,3584]{4,3,2,1,0:T(8,128)(2,1)S(1)} %bitcast.57, bf16[4,2,2,32,3584]{4,3,2,1,0:T(8,128)(2,1)S(1)} %bitcast.58, bf16[4,2,2,32,3584]{4,3,2,1,0:T(8,128)(2,1)S(1)} %bitcast.59, ...), custom_call_target="tpu_custom_call" | custom-call | flops 117440512 | bytes 3670016 | tf_op jit(solution)/shard_map/slopes/pallas_call | solution.py:135
  18.3 1.0 %collective-permute-start.8 = (bf16[32,2048]{1,0:T(8,128)(2,1)S(1)}, bf16[32,2048]{1,0:T(8,128)(2,1)S(1)}, u32[]{:S(2)}, u32[]{:S(2)}) collective-permute-start(bf16[32,2048]{1,0:T(8,128)(2,1)S(1)} %held.6), channel_id=1, source_target_pairs={{0,4},{4,0},{8,12},{12,8},{1,5},{5,1},{9,13},{13,9},{2,6},{6,2},{1... | collective-permute-start | bytes 393224 | tf_op jit(solution)/shard_map/ppermute | solution.py:18
  19.3 3.5 %collective-permute-start.9 = (bf16[32,2048]{1,0:T(8,128)(2,1)S(1)}, bf16[32,2048]{1,0:T(8,128)(2,1)S(1)}, u32[]{:S(2)}, u32[]{:S(2)}) collective-permute-start(bf16[32,2048]{1,0:T(8,128)(2,1)S(1)} %held.6), channel_id=1, source_target_pairs={{0,8},{4,12},{8,0},{12,4},{1,9},{5,13},{9,1},{13,5},{2,10},{6,14},... | collective-permute-start | bytes 393224 | tf_op jit(solution)/shard_map/ppermute | solution.py:18
  23.0 1.6 %collective-permute-done.3 = bf16[96,2048]{1,0:T(8,128)(2,1)S(1)} collective-permute-done((bf16[96,2048]{1,0:T(8,128)(2,1)S(1)}, bf16[96,2048]{1,0:T(8,128)(2,1)S(1)}, u32[]{:S(2)}, u32[]{:S(2)}) %collective-permute-start.3) | collective-permute-done | bytes 393248 | tf_op jit(solution)/shard_map/ppermute | solution.py:18
  24.7 12.4 %expert.2 = (f32[128,2176]{1,0:T(8,128)S(1)}, bf16[128,2176]{1,0:T(8,128)(2,1)S(1)}) custom-call(bf16[256,2048]{1,0:T(8,128)(2,1)S(1)} %slice_dynamic-update-slice_fusion.3.rows_ref, bf16[3584,256]{1,0:T(8,128)(2,1)S(1)} %get-tuple-element.22.slope_ref, f32[256,64]{1,0:T(8,128)S(1)} %get-tuple-element.23.down_part_ref, bf16[64,3584]{1,0:T(8,128)(2,1)S(1)} %bitcast.67, ...), custom_call_target="tpu_custom_call" | custom-call | flops 7516192768 | bytes 29360128 | tf_op jit(solution)/shard_map/expert/pallas_call | solution.py:233
  38.0 1.1 %collective-permute-done.11 = bf16[96,2048]{1,0:T(8,128)(2,1)S(1)} collective-permute-done((bf16[96,2048]{1,0:T(8,128)(2,1)S(1)}, bf16[96,2048]{1,0:T(8,128)(2,1)S(1)}, u32[]{:S(2)}, u32[]{:S(2)}) %collective-permute-start.11) | collective-permute-done | bytes 393248 | tf_op jit(solution)/shard_map/ppermute | solution.py:18
  40.6 3.8 %collective-permute-start.6 = (bf16[32,2176]{1,0:T(8,128)(2,1)S(1)}, bf16[32,2176]{1,0:T(8,128)(2,1)S(1)}, u32[]{:S(2)}, u32[]{:S(2)}) collective-permute-start(bf16[32,2176]{1,0:T(8,128)(2,1)S(1)} %get-tuple-element.28.refs_1_), channel_id=1, source_target_pairs={{0,8},{4,12},{8,0},{12,4},{1,9},{5,13},{9,1},{13,5},{2,10},{6,14},... | collective-permute-start | bytes 417800 | tf_op jit(solution)/shard_map/ppermute | solution.py:18
  44.4 12.4 %expert.3 = (f32[128,2176]{1,0:T(8,128)S(1)}, bf16[128,2176]{1,0:T(8,128)(2,1)S(1)}) custom-call(bf16[256,2048]{1,0:T(8,128)(2,1)S(1)} %slice_dynamic-update-slice_fusion.rows_ref, bf16[3584,256]{1,0:T(8,128)(2,1)S(1)} %get-tuple-element.31.slope_ref, f32[256,64]{1,0:T(8,128)S(1)} %get-tuple-element.32.down_part_ref, bf16[64,3584]{1,0:T(8,128)(2,1)S(1)} %bitcast.68, ...), custom_call_target="tpu_custom_call" | custom-call | flops 7516192768 | bytes 29360128 | tf_op jit(solution)/shard_map/expert/pallas_call | solution.py:233
  57.3 1.3 %fusion = f32[128,64]{0,1:T(8,128)S(1)} fusion(bf16[1,128,2048]{2,1,0:T(8,128)(2,1)} %param.10, bf16[1,2048,64]{1,2,0:T(8,128)(2,1)S(1)} %copy-done), kind=kOutput, calls=%fused_computation.3 | convolution fusion | flops 33554432 | bytes 819200 | tf_op jit(solution)/shard_map/dot_general | solution.py:353
  60.1 3.7 %collective-permute-start.15 = (bf16[32,2176]{1,0:T(8,128)(2,1)S(1)}, bf16[32,2176]{1,0:T(8,128)(2,1)S(1)}, u32[]{:S(2)}, u32[]{:S(2)}) collective-permute-start(bf16[32,2176]{1,0:T(8,128)(2,1)S(1)} %get-tuple-element.37), channel_id=1, source_target_pairs={{0,8},{4,12},{8,0},{12,4},{1,9},{5,13},{9,1},{13,5},{2,10},{6,14},... | collective-permute-start | bytes 417800 | tf_op jit(solution)/shard_map/ppermute | solution.py:18
  63.8 3.4 %collective-permute-done.13.refs_0_ = bf16[32,2176]{1,0:T(8,128)(2,1)S(1)} collective-permute-done((bf16[32,2176]{1,0:T(8,128)(2,1)S(1)}, bf16[32,2176]{1,0:T(8,128)(2,1)S(1)}, u32[]{:S(2)}, u32[]{:S(2)}) %collective-permute-start.13) | collective-permute-done | bytes 139296 | tf_op jit(solution)/shard_map/ppermute | solution.py:18
  67.2 1.9 %collective-permute-start.14 = (bf16[32,2048]{1,0:T(8,128)(2,1)S(1)}, bf16[32,2048]{1,0:T(8,128)(2,1)S(1)}, u32[]{:S(2)}, u32[]{:S(2)}) collective-permute-start(bf16[32,2048]{1,0:T(8,128)(2,1)S(1)} %held.11), channel_id=1, source_target_pairs={{0,2},{2,0},{1,3},{3,1},{4,6},{6,4},{5,7},{7,5},{8,10},{10,8},{9,1... | collective-permute-start | bytes 393224 | tf_op jit(solution)/shard_map/ppermute | solution.py:289
  69.2 5.1 %collective-permute-done.15.refs_1_ = bf16[32,2176]{1,0:T(8,128)(2,1)S(1)} collective-permute-done((bf16[32,2176]{1,0:T(8,128)(2,1)S(1)}, bf16[32,2176]{1,0:T(8,128)(2,1)S(1)}, u32[]{:S(2)}, u32[]{:S(2)}) %collective-permute-start.15) | collective-permute-done | bytes 139296 | tf_op jit(solution)/shard_map/ppermute | solution.py:18
  74.6 1.6 %collective-permute-start.17 = (bf16[32,2048]{1,0:T(8,128)(2,1)S(1)}, bf16[32,2048]{1,0:T(8,128)(2,1)S(1)}, u32[]{:S(2)}, u32[]{:S(2)}) collective-permute-start(bf16[32,2048]{1,0:T(8,128)(2,1)S(1)} %get-tuple-element.39), channel_id=1, source_target_pairs={{0,2},{2,0},{1,3},{3,1},{4,6},{6,4},{5,7},{7,5},{8,10},{10,8},{9,1... | collective-permute-start | bytes 393224 | tf_op jit(solution)/shard_map/ppermute | solution.py:289
  77.9 2.7 %collective-permute-done.17 = bf16[32,2048]{1,0:T(8,128)(2,1)S(1)} collective-permute-done((bf16[32,2048]{1,0:T(8,128)(2,1)S(1)}, bf16[32,2048]{1,0:T(8,128)(2,1)S(1)}, u32[]{:S(2)}, u32[]{:S(2)}) %collective-permute-start.17) | collective-permute-done | bytes 131104 | tf_op jit(solution)/shard_map/ppermute | solution.py:289
  80.6 1.3 %collective-permute-done.19 = bf16[32,2048]{1,0:T(8,128)(2,1)S(1)} collective-permute-done((bf16[32,2048]{1,0:T(8,128)(2,1)S(1)}, bf16[32,2048]{1,0:T(8,128)(2,1)S(1)}, u32[]{:S(2)}, u32[]{:S(2)}) %collective-permute-start.19) | collective-permute-done | bytes 131104 | tf_op jit(solution)/shard_map/ppermute | solution.py:18
  81.9 0.8 %maximum_bitcast_fusion = bf16[1,128,2048]{2,1,0:T(8,128)(2,1)} fusion(bf16[64,2048]{1,0:T(8,128)(2,1)S(1)} %get-tuple-element.45, bf16[64,2048]{1,0:T(8,128)(2,1)S(1)} %get-tuple-element.44), kind=kLoop, calls=%fused_computation.2 | loop fusion | flops 1048576 | bytes 1048576 | tf_op jit(solution)/shard_map/broadcast_in_dim | solution.py:373
  (92 shorter events, 7.4 us)
Async XLA Ops:
  0.6 56.7 %copy-start = (bf16[1,2048,64]{1,2,0:T(8,128)(2,1)S(1)}, bf16[1,2048,64]{1,2,0:T(8,128)(2,1)}, u32[]{:S(2)}) copy-start(bf16[1,2048,64]{1,2,0:T(8,128)(2,1)} %param.17) | copy-start | bytes 786436
  1.6 16.7 %collective-permute-start = (bf16[32,2048]{1,0:T(8,128)(2,1)S(1)}, bf16[32,2048]{1,0:T(8,128)(2,1)S(1)}, u32[]{:S(2)}, u32[]{:S(2)}) collective-permute-start(bf16[32,2048]{1,0:T(8,128)(2,1)S(1)} %get-tuple-element.43.cot_ref), channel_id=1, source_target_pairs={{0,4},{4,0},{8,12},{12,8},{1,5},{5,1},{9,13},{13,9},{2,6},{6,2},{1... | collective-permute-start | bytes 393224 | tf_op jit(solution)/shard_map/ppermute | solution.py:18
  4.7 18.1 %collective-permute-start.1 = (bf16[32,2048]{1,0:T(8,128)(2,1)S(1)}, bf16[32,2048]{1,0:T(8,128)(2,1)S(1)}, u32[]{:S(2)}, u32[]{:S(2)}) collective-permute-start(bf16[32,2048]{1,0:T(8,128)(2,1)S(1)} %get-tuple-element.43.cot_ref), channel_id=1, source_target_pairs={{0,8},{4,12},{8,0},{12,4},{1,9},{5,13},{9,1},{13,5},{2,10},{6,14},... | collective-permute-start | bytes 393224 | tf_op jit(solution)/shard_map/ppermute | solution.py:18
  7.3 15.5 %collective-permute-start.2 = (bf16[32,2048]{1,0:T(8,128)(2,1)S(1)}, bf16[32,2048]{1,0:T(8,128)(2,1)S(1)}, u32[]{:S(2)}, u32[]{:S(2)}) collective-permute-start(bf16[32,2048]{1,0:T(8,128)(2,1)S(1)} %get-tuple-element.43.cot_ref), channel_id=1, source_target_pairs={{0,12},{4,8},{8,4},{12,0},{1,13},{5,9},{9,5},{13,1},{2,14},{6,10},... | collective-permute-start | bytes 393224 | tf_op jit(solution)/shard_map/ppermute | solution.py:18
  18.3 18.8 %collective-permute-start.8 = (bf16[32,2048]{1,0:T(8,128)(2,1)S(1)}, bf16[32,2048]{1,0:T(8,128)(2,1)S(1)}, u32[]{:S(2)}, u32[]{:S(2)}) collective-permute-start(bf16[32,2048]{1,0:T(8,128)(2,1)S(1)} %held.6), channel_id=1, source_target_pairs={{0,4},{4,0},{8,12},{12,8},{1,5},{5,1},{9,13},{13,9},{2,6},{6,2},{1... | collective-permute-start | bytes 393224 | tf_op jit(solution)/shard_map/ppermute | solution.py:18
  19.3 17.9 %collective-permute-start.9 = (bf16[32,2048]{1,0:T(8,128)(2,1)S(1)}, bf16[32,2048]{1,0:T(8,128)(2,1)S(1)}, u32[]{:S(2)}, u32[]{:S(2)}) collective-permute-start(bf16[32,2048]{1,0:T(8,128)(2,1)S(1)} %held.6), channel_id=1, source_target_pairs={{0,8},{4,12},{8,0},{12,4},{1,9},{5,13},{9,1},{13,5},{2,10},{6,14},... | collective-permute-start | bytes 393224 | tf_op jit(solution)/shard_map/ppermute | solution.py:18
  22.8 14.4 %collective-permute-start.10 = (bf16[32,2048]{1,0:T(8,128)(2,1)S(1)}, bf16[32,2048]{1,0:T(8,128)(2,1)S(1)}, u32[]{:S(2)}, u32[]{:S(2)}) collective-permute-start(bf16[32,2048]{1,0:T(8,128)(2,1)S(1)} %held.6), channel_id=1, source_target_pairs={{0,12},{4,8},{8,4},{12,0},{1,13},{5,9},{9,5},{13,1},{2,14},{6,10},... | collective-permute-start | bytes 393224 | tf_op jit(solution)/shard_map/ppermute | solution.py:18
  22.9 1.8 %collective-permute-start.3 = (bf16[96,2048]{1,0:T(8,128)(2,1)S(1)}, bf16[96,2048]{1,0:T(8,128)(2,1)S(1)}, u32[]{:S(2)}, u32[]{:S(2)}) collective-permute-start(bf16[96,2048]{1,0:T(8,128)(2,1)S(1)} %pad_maximum_fusion), channel_id=1, source_target_pairs={{0,1},{1,0},{2,3},{3,2},{4,5},{5,4},{6,7},{7,6},{8,9},{9,8},{10,11... | collective-permute-start | bytes 1179656 | tf_op jit(solution)/shard_map/ppermute | solution.py:18
  37.3 1.8 %collective-permute-start.11 = (bf16[96,2048]{1,0:T(8,128)(2,1)S(1)}, bf16[96,2048]{1,0:T(8,128)(2,1)S(1)}, u32[]{:S(2)}, u32[]{:S(2)}) collective-permute-start(bf16[96,2048]{1,0:T(8,128)(2,1)S(1)} %pad_maximum_fusion.1), channel_id=1, source_target_pairs={{0,1},{1,0},{2,3},{3,2},{4,5},{5,4},{6,7},{7,6},{8,9},{9,8},{10,11... | collective-permute-start | bytes 1179656 | tf_op jit(solution)/shard_map/ppermute | solution.py:18
  37.5 2.4 %collective-permute-start.4 = (bf16[128,2176]{1,0:T(8,128)(2,1)S(1)}, bf16[128,2176]{1,0:T(8,128)(2,1)S(1)}, u32[]{:S(2)}, u32[]{:S(2)}) collective-permute-start(bf16[128,2176]{1,0:T(8,128)(2,1)S(1)} %get-tuple-element.25), channel_id=1, source_target_pairs={{0,1},{1,0},{2,3},{3,2},{4,5},{5,4},{6,7},{7,6},{8,9},{9,8},{10,11... | collective-permute-start | bytes 1671176 | tf_op jit(solution)/shard_map/ppermute | solution.py:18
  40.0 16.9 %collective-permute-start.5 = (bf16[32,2176]{1,0:T(8,128)(2,1)S(1)}, bf16[32,2176]{1,0:T(8,128)(2,1)S(1)}, u32[]{:S(2)}, u32[]{:S(2)}) collective-permute-start(bf16[32,2176]{1,0:T(8,128)(2,1)S(1)} %get-tuple-element.27.refs_0_), channel_id=1, source_target_pairs={{0,4},{4,0},{8,12},{12,8},{1,5},{5,1},{9,13},{13,9},{2,6},{6,2},{1... | collective-permute-start | bytes 417800 | tf_op jit(solution)/shard_map/ppermute | solution.py:18
  40.6 16.3 %collective-permute-start.6 = (bf16[32,2176]{1,0:T(8,128)(2,1)S(1)}, bf16[32,2176]{1,0:T(8,128)(2,1)S(1)}, u32[]{:S(2)}, u32[]{:S(2)}) collective-permute-start(bf16[32,2176]{1,0:T(8,128)(2,1)S(1)} %get-tuple-element.28.refs_1_), channel_id=1, source_target_pairs={{0,8},{4,12},{8,0},{12,4},{1,9},{5,13},{9,1},{13,5},{2,10},{6,14},... | collective-permute-start | bytes 417800 | tf_op jit(solution)/shard_map/ppermute | solution.py:18
  44.4 12.5 %collective-permute-start.7 = (bf16[32,2176]{1,0:T(8,128)(2,1)S(1)}, bf16[32,2176]{1,0:T(8,128)(2,1)S(1)}, u32[]{:S(2)}, u32[]{:S(2)}) collective-permute-start(bf16[32,2176]{1,0:T(8,128)(2,1)S(1)} %get-tuple-element.29.refs_2_), channel_id=1, source_target_pairs={{0,12},{4,8},{8,4},{12,0},{1,13},{5,9},{9,5},{13,1},{2,14},{6,10},... | collective-permute-start | bytes 417800 | tf_op jit(solution)/shard_map/ppermute | solution.py:18
  44.4 12.8 %copy-start.7 = (s32[1,1,4]{2,1,0:T(1,128)S(1)}, s32[1,1,4]{2,1,0:T(1,128)}, u32[]{:S(2)}) copy-start(s32[1,1,4]{2,1,0:T(1,128)} %param.19) | copy-start | bytes 52
  56.9 2.0 %collective-permute-start.12 = (bf16[128,2176]{1,0:T(8,128)(2,1)S(1)}, bf16[128,2176]{1,0:T(8,128)(2,1)S(1)}, u32[]{:S(2)}, u32[]{:S(2)}) collective-permute-start(bf16[128,2176]{1,0:T(8,128)(2,1)S(1)} %held.10), channel_id=1, source_target_pairs={{0,1},{1,0},{2,3},{3,2},{4,5},{5,4},{6,7},{7,6},{8,9},{9,8},{10,11... | collective-permute-start | bytes 1671176 | tf_op jit(solution)/shard_map/ppermute | solution.py:18
  59.1 17.4 %copy-start.5 = (f32[1,128,64]{1,2,0:T(8,128)S(1)}, f32[1,128,64]{1,2,0:T(8,128)}, u32[]{:S(2)}) copy-start(f32[1,128,64]{1,2,0:T(8,128)} %param.16) | copy-start | bytes 98308
  59.1 8.1 %collective-permute-start.13 = (bf16[32,2176]{1,0:T(8,128)(2,1)S(1)}, bf16[32,2176]{1,0:T(8,128)(2,1)S(1)}, u32[]{:S(2)}, u32[]{:S(2)}) collective-permute-start(bf16[32,2176]{1,0:T(8,128)(2,1)S(1)} %get-tuple-element.35), channel_id=1, source_target_pairs={{0,4},{4,0},{8,12},{12,8},{1,5},{5,1},{9,13},{13,9},{2,6},{6,2},{1... | collective-permute-start | bytes 417800 | tf_op jit(solution)/shard_map/ppermute | solution.py:18
  60.1 14.2 %collective-permute-start.15 = (bf16[32,2176]{1,0:T(8,128)(2,1)S(1)}, bf16[32,2176]{1,0:T(8,128)(2,1)S(1)}, u32[]{:S(2)}, u32[]{:S(2)}) collective-permute-start(bf16[32,2176]{1,0:T(8,128)(2,1)S(1)} %get-tuple-element.37), channel_id=1, source_target_pairs={{0,8},{4,12},{8,0},{12,4},{1,9},{5,13},{9,1},{13,5},{2,10},{6,14},... | collective-permute-start | bytes 417800 | tf_op jit(solution)/shard_map/ppermute | solution.py:18
  63.8 10.5 %collective-permute-start.16 = (bf16[32,2176]{1,0:T(8,128)(2,1)S(1)}, bf16[32,2176]{1,0:T(8,128)(2,1)S(1)}, u32[]{:S(2)}, u32[]{:S(2)}) collective-permute-start(bf16[32,2176]{1,0:T(8,128)(2,1)S(1)} %get-tuple-element.38), channel_id=1, source_target_pairs={{0,12},{4,8},{8,4},{12,0},{1,13},{5,9},{9,5},{13,1},{2,14},{6,10},... | collective-permute-start | bytes 417800 | tf_op jit(solution)/shard_map/ppermute | solution.py:18
  67.2 7.1 %collective-permute-start.14 = (bf16[32,2048]{1,0:T(8,128)(2,1)S(1)}, bf16[32,2048]{1,0:T(8,128)(2,1)S(1)}, u32[]{:S(2)}, u32[]{:S(2)}) collective-permute-start(bf16[32,2048]{1,0:T(8,128)(2,1)S(1)} %held.11), channel_id=1, source_target_pairs={{0,2},{2,0},{1,3},{3,1},{4,6},{6,4},{5,7},{7,5},{8,10},{10,8},{9,1... | collective-permute-start | bytes 393224 | tf_op jit(solution)/shard_map/ppermute | solution.py:289
  74.5 1.8 %collective-permute-start.20 = (f32[64,128]{1,0:T(8,128)S(1)}, f32[64,128]{1,0:T(8,128)S(1)}, u32[]{:S(2)}, u32[]{:S(2)}) collective-permute-start(f32[64,128]{1,0:T(8,128)S(1)} %constant_dynamic-update-slice_fusion.12), channel_id=1, source_target_pairs={{0,1},{1,0},{2,3},{3,2},{4,5},{5,4},{6,7},{7,6},{8,9},{9,8},{10,11... | collective-permute-start | bytes 98312 | tf_op jit(solution)/shard_map/ppermute | solution.py:18
  74.6 5.9 %collective-permute-start.17 = (bf16[32,2048]{1,0:T(8,128)(2,1)S(1)}, bf16[32,2048]{1,0:T(8,128)(2,1)S(1)}, u32[]{:S(2)}, u32[]{:S(2)}) collective-permute-start(bf16[32,2048]{1,0:T(8,128)(2,1)S(1)} %get-tuple-element.39), channel_id=1, source_target_pairs={{0,2},{2,0},{1,3},{3,1},{4,6},{6,4},{5,7},{7,5},{8,10},{10,8},{9,1... | collective-permute-start | bytes 393224 | tf_op jit(solution)/shard_map/ppermute | solution.py:289
  76.2 4.4 %collective-permute-start.18 = (bf16[32,2048]{1,0:T(8,128)(2,1)S(1)}, bf16[32,2048]{1,0:T(8,128)(2,1)S(1)}, u32[]{:S(2)}, u32[]{:S(2)}) collective-permute-start(bf16[32,2048]{1,0:T(8,128)(2,1)S(1)} %collective-permute-done.14.refs_3_), channel_id=1, source_target_pairs={{0,1},{1,0},{2,3},{3,2},{4,5},{5,4},{6,7},{7,6},{8,9},{9,8},{10,11... | collective-permute-start | bytes 393224 | tf_op jit(solution)/shard_map/ppermute | solution.py:18
  80.5 1.3 %collective-permute-start.19 = (bf16[32,2048]{1,0:T(8,128)(2,1)S(1)}, bf16[32,2048]{1,0:T(8,128)(2,1)S(1)}, u32[]{:S(2)}, u32[]{:S(2)}) collective-permute-start(bf16[32,2048]{1,0:T(8,128)(2,1)S(1)} %collective-permute-done.17), channel_id=1, source_target_pairs={{0,1},{1,0},{2,3},{3,2},{4,5},{5,4},{6,7},{7,6},{8,9},{9,8},{10,11... | collective-permute-start | bytes 393224 | tf_op jit(solution)/shard_map/ppermute | solution.py:18
  (5 other events, 17.4 us)
